TPU v7x, 32 devices: a whole 2x2x4 slice. The times are simulated.
32 devices in a mesh: sub: 8 (over z, x), grp: 4 (over y, core).
Axes of the slice: x: 2, y: 2, z: 4, core: 2. Of those that a mesh axis runs over, the one named last changes fastest.
Arguments:
- loads: float32 [4, 16, 2, 48, 256], P('grp', 'sub'), may hold values from -18 to 18
- inv_schur: bfloat16 [4, 16, 1024, 1024], P('grp', 'sub'), as said below
- schur: bfloat16 [4, 16, 1024, 1024], P('grp', 'sub'), as said below
- coarse_map: bfloat16 [4, 16, 12, 1024], P('grp', 'sub'), may hold values from -0.75 to 0.75
- coarse_inverse: float32 [4, 16, 12, 4, 192], P('grp', 'sub'), as said below
- face_rows: int32 [4, 16, 1024], P('grp', 'sub'), may hold values from 0 to 1023, each once within a row
- face_len: int32 [4, 16, 2], P('grp', 'sub'), may hold values from 64 to 256
Outputs:
- multipliers: float32 [4, 16, 2, 48, 256], P('grp', 'sub')
- residual: float32 [4, 16, 2, 48, 256], P('grp', 'sub')
Inputs may be any that keep to these rules, and one draw needn't show every extreme that they name: `inv_schur`: each subdomain's matrix is symmetric and positive definite. `schur`: each subdomain's matrix is symmetric and positive definite. `coarse_inverse`: seen as a [768, 768] matrix it is symmetric and positive definite. `face_rows`: each subdomain's row is a permutation of 0 to 1023.
All inputs are finite; a program needn't handle non-finite values.
Results may differ from a plain program's by a relative error of at most 0.025.
Values sent between devices are 32-bit elements; how exact they have to be, the bound alone decides.
A program may use at most 128 MiB of HBM per device.

v0:
```python
import jax
import jax.numpy as jnp
from jax import lax
from jax.sharding import PartitionSpec as P

FACE = 256
LOADS = 48
CDOF = 12
ITERS = 3


def shifted(value, axis, steps):
    count = lax.axis_size(axis)
    initial, last = (max(0, -steps), min(count, count - steps))
    return lax.ppermute(value, axis, [(source, source + steps) for source in range(initial, last)])


def passed_along(block, axis, distance):
    devices = range(lax.axis_size(axis))
    route = [((i - distance) % len(devices), i) for i in devices]
    return lax.ppermute(block, axis, route)


def pair_sum(first, second, pattern):
    return jnp.einsum(pattern, first, second, precision=lax.Precision.HIGHEST)


def combine(weights, faces):
    return jnp.einsum("ab,gksat->gksbt", weights, faces, precision=lax.Precision.HIGHEST)


def gram_solve(matrix, right):
    return jax.scipy.linalg.cho_solve((jnp.linalg.cholesky(matrix), True), right)


def to_slots(faces):
    along = faces[0, :, 0]
    beside_all = faces[0, :, 1]
    from_left = shifted(along[1:2], "sub", 1)
    from_left = jnp.concatenate([from_left, along[0:1]], axis=0)
    from_below = passed_along(beside_all, "grp", 1)
    stacked = jnp.stack([-from_left, along, -from_below, beside_all], axis=2)
    return stacked.reshape(stacked.shape[0], stacked.shape[1], -1)


def to_faces(field, live_mask):
    pieces = field.reshape(field.shape[0], field.shape[1], 4, -1)
    from_right = shifted(pieces[0:1, :, 0], "sub", -1)
    neighbour = jnp.concatenate([pieces[1:2, :, 0], from_right], axis=0)
    from_above = passed_along(pieces[:, :, 2], "grp", -1)
    jumps = jnp.stack([pieces[:, :, 1] - neighbour, pieces[:, :, 3] - from_above], axis=1)
    return jumps[None] * live_mask


def body(loads, inv_schur, schur, coarse_map, coarse_inverse, face_rows, face_len):
    slot_rows = face_rows[0]
    permute = jax.vmap(lambda matrix, ordering: matrix[ordering][:, ordering])
    solve_mats = permute(inv_schur[0], slot_rows)
    dirichlet = permute(schur[0], slot_rows)
    coarse_basis = jax.vmap(lambda basis_rows, ordering: basis_rows[:, ordering])(
        coarse_map[0], slot_rows
    )
    own_rows = coarse_inverse[0].reshape(2 * CDOF, coarse_inverse.shape[3], coarse_inverse.shape[4])
    positions = jnp.arange(FACE)
    column = 2 * lax.axis_index("sub") + jnp.arange(2)
    last_column = 2 * lax.axis_size("sub") - 1
    along_live = (positions[None, :] < face_len[0, :, 0:1]) & (column[:, None] < last_column)
    around_live = positions[None, :] < face_len[0, :, 1:2]
    live_mask = jnp.stack([along_live, around_live], axis=1).astype(jnp.float32)[
        None, :, :, None, :
    ]

    def precondition(resid):
        slotted = to_slots(resid)
        smoothed = jnp.einsum(
            "krm,kmn->krn",
            slotted.astype(jnp.bfloat16),
            dirichlet,
            preferred_element_type=jnp.float32,
        )
        filtered = to_faces(smoothed, live_mask)
        product = lax.psum(pair_sum(filtered, resid, "gksat,gksbt->ab"), ("sub", "grp"))
        return (filtered, product)

    residual = loads * live_mask
    multipliers = jnp.zeros_like(residual)
    search, precond_gram = precondition(residual)
    direction = search
    for iteration in range(ITERS):
        operator_slotted = to_slots(direction)
        rounded = operator_slotted.astype(jnp.bfloat16)
        local_part = jnp.einsum(
            "krm,kmn->krn", rounded, solve_mats, preferred_element_type=jnp.float32
        )
        operator_coarse_terms = jnp.einsum(
            "krm,kqm->krq", rounded, coarse_basis, preferred_element_type=jnp.float32
        )
        flat_terms = jnp.transpose(operator_coarse_terms, (1, 0, 2)).reshape(1, LOADS, 2 * CDOF)
        cycle_terms = lax.all_gather(flat_terms, "grp", axis=0, tiled=True)
        solved = jnp.einsum(
            "grx,kgx->rk",
            lax.all_gather(cycle_terms, "sub", axis=2, tiled=True),
            own_rows,
            precision=lax.Precision.HIGHEST,
        )
        corrections = jnp.transpose(solved.reshape(LOADS, 2, CDOF), (1, 0, 2)).astype(jnp.bfloat16)
        response = local_part + jnp.einsum(
            "krq,kqm->krm", corrections, coarse_basis, preferred_element_type=jnp.float32
        )
        image_faces = to_faces(response, live_mask)
        curvature = lax.psum(pair_sum(direction, image_faces, "gksat,gksbt->ab"), ("sub", "grp"))
        image_faces, curvature = (image_faces, curvature)
        step_size = gram_solve(curvature, precond_gram)
        multipliers = multipliers + combine(step_size, direction)
        residual = residual - combine(step_size, image_faces)
        if iteration + 1 < ITERS:
            search, new_gram = precondition(residual)
            conjugate = gram_solve(precond_gram, new_gram)
            direction = search + combine(conjugate, direction)
            precond_gram = new_gram
    return (multipliers, residual)


def solution(mesh):
    in_specs = (
        P("grp", "sub", None, None, None),
        P("grp", "sub", None, None),
        P("grp", "sub", None, None),
        P("grp", "sub", None, None),
        P("grp", "sub", None, None, None),
        P("grp", "sub", None),
        P("grp", "sub", None),
    )
    out_specs = (P("grp", "sub", None, None, None), P("grp", "sub", None, None, None))
    return jax.shard_map(body, mesh=mesh, in_specs=in_specs, out_specs=out_specs, check_vma=False)
```

profile of v0, /device:TPU:10, one launch (start us, length us, event | category | flops | bytes accessed | tf_op | source)
XLA Modules:
  0.0 658.3 jit_solution(1124318638356162383)
XLA Ops:
  7.0 41.9 %gather_fusion = bf16[2048,1024]{1,0:T(8,128)(2,1)} fusion(bf16[2,1024,1024]{2,1,0:T(8,128)(2,1)} %bitcast.533, s32[2048]{0:T(1024)S(1)} %bitcast.528), kind=kCustom, calls=%fused_computation | custom fusion | bytes 8404992 | tf_op jit(solution)/shard_map/vmap()/gather | solution.py:57
  48.9 6.2 copy.171
  55.2 40.3 %gather_fusion.1 = bf16[2048,1024]{1,0:T(8,128)(2,1)} fusion(bf16[2,1024,1024]{1,2,0:T(8,128)(2,1)} %copy.171, s32[2048]{0:T(1024)S(1)} %bitcast.529), kind=kCustom, calls=%fused_computation.1 | custom fusion | bytes 8404992 | tf_op jit(solution)/shard_map/vmap()/gather | solution.py:57
  95.5 42.0 %gather_fusion.2 = bf16[2048,1024]{1,0:T(8,128)(2,1)} fusion(bf16[2,1024,1024]{2,1,0:T(8,128)(2,1)} %bitcast.534, s32[2048]{0:T(1024)S(1)} %bitcast.530), kind=kCustom, calls=%fused_computation.2 | custom fusion | bytes 8404992 | tf_op jit(solution)/shard_map/vmap()/gather | solution.py:57
  137.5 6.2 copy.182
  143.8 40.4 %gather_fusion.3 = bf16[2048,1024]{1,0:T(8,128)(2,1)} fusion(bf16[2,1024,1024]{1,2,0:T(8,128)(2,1)} %copy.182, s32[2048]{0:T(1024)S(1)} %bitcast.531), kind=kCustom, calls=%fused_computation.3 | custom fusion | bytes 8404992 | tf_op jit(solution)/shard_map/vmap()/gather | solution.py:57
  184.5 11.1 %gather_fusion.4 = bf16[2048,12]{1,0:T(8,128)(2,1)S(1)} fusion(bf16[2,12,1024]{1,2,0:T(8,128)(2,1)S(1)} %bitcast.549, s32[2048]{0:T(1024)S(1)} %bitcast.532), kind=kCustom, calls=%fused_computation.4 | custom fusion | bytes 114688 | tf_op jit(solution)/shard_map/vmap()/gather | solution.py:60
  216.7 5.2 all_gather.18
  221.9 26.2 %all_gather.19 = f32[4,48,192]{1,2,0:T(8,128)S(1)} all-gather(f32[4,48,24]{1,2,0:T(8,128)S(1)} %all_gather.18), channel_id=1, replica_groups=mesh['sub'=8,'grp'=4] {'sub'}, dimensions={2}, use_global_device_ids=true | all-gather | bytes 165888 | tf_op jit(solution)/shard_map/all_gather | solution.py:102
  256.8 43.6 %all-reduce = (f32[48,48]{0,1:T(8,128)S(1)}, f32[48,48]{0,1:T(8,128)S(1)}) all-reduce(f32[48,48]{0,1:T(8,128)S(1)} %convolution_bitcast_fusion.14, f32[48,48]{0,1:T(8,128)S(1)} %convolution_bitcast_fusion.15), channel_id=1, replica_groups=mesh['sub'=8,'grp'=4] {'sub','grp'}, use_global_device_ids=true, to_apply=%region_3.5 | all-reduce | flops 4608 | bytes 36864 | tf_op jit(solution)/shard_map/psum | solution.py:82
  300.6 4.4 cholesky.89
  313.2 4.4 cholesky.100
  334.8 40.7 %psum.44 = f32[48,48]{0,1:T(8,128)S(1)} all-reduce(f32[48,48]{0,1:T(8,128)S(1)} %convolution_bitcast_fusion.13), channel_id=1, replica_groups=mesh['sub'=8,'grp'=4] {'sub','grp'}, use_global_device_ids=true, to_apply=%region_4.0 | all-reduce | flops 2304 | bytes 18432 | tf_op jit(solution)/shard_map/psum | solution.py:82
  395.8 5.4 all_gather.20
  401.2 26.6 %all_gather.21 = f32[4,48,192]{1,2,0:T(8,128)S(1)} all-gather(f32[4,48,24]{1,2,0:T(8,128)S(1)} %all_gather.20), channel_id=1, replica_groups=mesh['sub'=8,'grp'=4] {'sub'}, dimensions={2}, use_global_device_ids=true | all-gather | bytes 165888 | tf_op jit(solution)/shard_map/all_gather | solution.py:102
  428.7 5.9 collective-permute-start.14
  437.8 43.5 %psum.45 = f32[48,48]{0,1:T(8,128)S(1)} all-reduce(f32[48,48]{0,1:T(8,128)S(1)} %convolution_bitcast_fusion.12), channel_id=1, replica_groups=mesh['sub'=8,'grp'=4] {'sub','grp'}, use_global_device_ids=true, to_apply=%region_5.0 | all-reduce | flops 2304 | bytes 18432 | tf_op jit(solution)/shard_map/psum | solution.py:111
  481.4 4.4 cholesky.111
  508.8 41.7 %psum.46 = f32[48,48]{1,0:T(8,128)S(1)} all-reduce(f32[48,48]{1,0:T(8,128)S(1)} %convolution_bitcast_fusion.11), channel_id=1, replica_groups=mesh['sub'=8,'grp'=4] {'sub','grp'}, use_global_device_ids=true, to_apply=%region_6.9 | all-reduce | flops 2304 | bytes 18432 | tf_op jit(solution)/shard_map/psum | solution.py:82
  561.3 5.4 all_gather.22
  566.7 26.5 %all_gather.23 = f32[4,48,192]{1,2,0:T(8,128)S(1)} all-gather(f32[4,48,24]{1,2,0:T(8,128)S(1)} %all_gather.22), channel_id=1, replica_groups=mesh['sub'=8,'grp'=4] {'sub'}, dimensions={2}, use_global_device_ids=true | all-gather | bytes 165888 | tf_op jit(solution)/shard_map/all_gather | solution.py:102
  594.2 5.9 collective-permute-start.22
  603.0 43.4 %psum.47 = f32[48,48]{0,1:T(8,128)S(1)} all-reduce(f32[48,48]{0,1:T(8,128)S(1)} %convolution_bitcast_fusion.10), channel_id=1, replica_groups=mesh['sub'=8,'grp'=4] {'sub','grp'}, use_global_device_ids=true, to_apply=%region_7.10 | all-reduce | flops 2304 | bytes 18432 | tf_op jit(solution)/shard_map/psum | solution.py:111
  646.4 4.4 cholesky.133
  (233 shorter events, 130.4 us)
Async XLA Ops:
  2.7 193.0 %collective-permute-start = (f32[1,48,256]{2,1,0:T(8,128)S(1)}, f32[1,48,256]{2,1,0:T(8,128)S(1)}, u32[]{:S(2)}, u32[]{:S(2)}) collective-permute-start(f32[1,48,256]{2,1,0:T(8,128)S(1)} %get-tuple-element.64), channel_id=1, source_target_pairs={{0,4},{4,8},{8,12},{12,16},{16,20},{20,24},{24,28},{1,5},{5,9},{9,... | collective-permute-start | bytes 147464 | tf_op jit(solution)/shard_map/ppermute | solution.py:15
  6.2 189.5 %collective-permute-start.1 = (f32[2,48,256]{2,1,0:T(8,128)S(1)}, f32[2,48,256]{2,1,0:T(8,128)S(1)}, u32[]{:S(2)}, u32[]{:S(2)}) collective-permute-start(f32[2,48,256]{2,1,0:T(8,128)S(1)} %slice_bitcast_fusion.5), channel_id=1, source_target_pairs={{3,0},{0,1},{1,2},{2,3},{7,4},{4,5},{5,6},{6,7},{11,8},{8,9},{9,10... | collective-permute-start | bytes 294920 | tf_op jit(solution)/shard_map/ppermute | solution.py:21
  199.6 7.1 %collective-permute-start.2 = (f32[1,48,256]{2,1,0:T(8,128)S(1)}, f32[1,48,256]{2,1,0:T(8,128)S(1)}, u32[]{:S(2)}, u32[]{:S(2)}) collective-permute-start(f32[1,48,256]{2,1,0:T(8,128)S(1)} %bitcast.587), channel_id=1, source_target_pairs={{4,0},{8,4},{12,8},{16,12},{20,16},{24,20},{28,24},{5,1},{9,5},{13... | collective-permute-start | bytes 147464 | tf_op jit(solution)/shard_map/ppermute | solution.py:15
  202.6 4.2 collective-permute-start.3
  206.9 6.2 collective-permute-start.4
  210.9 4.1 collective-permute-start.5
  249.1 6.9 %collective-permute-start.6 = (f32[1,48,256]{2,1,0:T(8,128)S(1)}, f32[1,48,256]{2,1,0:T(8,128)S(1)}, u32[]{:S(2)}, u32[]{:S(2)}) collective-permute-start(f32[1,48,256]{2,1,0:T(8,128)S(1)} %bitcast.588), channel_id=1, source_target_pairs={{4,0},{8,4},{12,8},{16,12},{20,16},{24,20},{28,24},{5,1},{9,5},{13... | collective-permute-start | bytes 147464 | tf_op jit(solution)/shard_map/ppermute | solution.py:15
  253.7 2.5 collective-permute-start.7
  311.2 11.4 %collective-permute-start.8 = (f32[1,48,256]{2,1,0:T(8,128)S(1)}, f32[1,48,256]{2,1,0:T(8,128)S(1)}, u32[]{:S(2)}, u32[]{:S(2)}) collective-permute-start(f32[1,48,256]{2,1,0:T(8,128)S(1)} %get-tuple-element.54), channel_id=1, source_target_pairs={{0,4},{4,8},{8,12},{12,16},{16,20},{20,24},{24,28},{1,5},{5,9},{9,... | collective-permute-start | bytes 147464 | tf_op jit(solution)/shard_map/ppermute | solution.py:15
  313.1 9.5 %collective-permute-start.9 = (f32[2,48,256]{2,1,0:T(8,128)S(1)}, f32[2,48,256]{2,1,0:T(8,128)S(1)}, u32[]{:S(2)}, u32[]{:S(2)}) collective-permute-start(f32[2,48,256]{2,1,0:T(8,128)S(1)} %slice_bitcast_fusion.3), channel_id=1, source_target_pairs={{3,0},{0,1},{1,2},{2,3},{7,4},{4,5},{5,6},{6,7},{11,8},{8,9},{9,10... | collective-permute-start | bytes 294920 | tf_op jit(solution)/shard_map/ppermute | solution.py:21
  326.6 6.9 %collective-permute-start.10 = (f32[1,48,256]{2,1,0:T(8,128)S(1)}, f32[1,48,256]{2,1,0:T(8,128)S(1)}, u32[]{:S(2)}, u32[]{:S(2)}) collective-permute-start(f32[1,48,256]{2,1,0:T(8,128)S(1)} %bitcast.589), channel_id=1, source_target_pairs={{4,0},{8,4},{12,8},{16,12},{20,16},{24,20},{28,24},{5,1},{9,5},{13... | collective-permute-start | bytes 147464 | tf_op jit(solution)/shard_map/ppermute | solution.py:15
  330.8 3.7 collective-permute-start.11
  381.6 6.3 collective-permute-start.12
  387.8 4.1 collective-permute-start.13
  428.7 7.7 %collective-permute-start.14 = (f32[1,48,256]{2,1,0:T(8,128)S(1)}, f32[1,48,256]{2,1,0:T(8,128)S(1)}, u32[]{:S(2)}, u32[]{:S(2)}) collective-permute-start(f32[1,48,256]{2,1,0:T(8,128)S(1)} %bitcast.590), channel_id=1, source_target_pairs={{4,0},{8,4},{12,8},{16,12},{20,16},{24,20},{28,24},{5,1},{9,5},{13... | collective-permute-start | bytes 147464 | tf_op jit(solution)/shard_map/ppermute | solution.py:15
  434.9 2.5 collective-permute-start.15
  491.6 6.0 collective-permute-start.16
  493.5 4.1 collective-permute-start.17
  501.5 6.9 %collective-permute-start.18 = (f32[1,48,256]{2,1,0:T(8,128)S(1)}, f32[1,48,256]{2,1,0:T(8,128)S(1)}, u32[]{:S(2)}, u32[]{:S(2)}) collective-permute-start(f32[1,48,256]{2,1,0:T(8,128)S(1)} %bitcast.591), channel_id=1, source_target_pairs={{4,0},{8,4},{12,8},{16,12},{20,16},{24,20},{28,24},{5,1},{9,5},{13... | collective-permute-start | bytes 147464 | tf_op jit(solution)/shard_map/ppermute | solution.py:15
  505.8 2.7 collective-permute-start.19
  551.3 6.0 collective-permute-start.20
  553.3 4.1 collective-permute-start.21
  594.2 7.6 %collective-permute-start.22 = (f32[1,48,256]{2,1,0:T(8,128)S(1)}, f32[1,48,256]{2,1,0:T(8,128)S(1)}, u32[]{:S(2)}, u32[]{:S(2)}) collective-permute-start(f32[1,48,256]{2,1,0:T(8,128)S(1)} %bitcast.592), channel_id=1, source_target_pairs={{4,0},{8,4},{12,8},{16,12},{20,16},{24,20},{28,24},{5,1},{9,5},{13... | collective-permute-start | bytes 147464 | tf_op jit(solution)/shard_map/ppermute | solution.py:15
  600.4 2.3 collective-permute-start.23
  (3 other events, 303.4 us)
where the time goes:
time: 662 us; the launch traced here: 658 us
  blocking collectives  308 us (47%)
  local copies, waits for them, and re-layouts  193 us (29%)
  other arithmetic  49.2 us (7%)
  starting transfers between devices  47 us (7%)
  matrix products  30.1 us (5%)
  waiting for transfers between devices  28.4 us (4%)
    gather x6, local copies, waits for them, and re-layouts, body(): permute = jax.vmap(lambda matrix, ordering: matrix[ordering][:, ordering])  177 us
    psum x3, blocking collectives, precondition(): lax.psum(pair_sum(filtered, resid, 'gksat,gksbt->ab'), ('sub', 'grp'))  126 us
    psum x2, blocking collectives, body(): lax.psum(pair_sum(direction, image_faces, 'gksat,gksbt->ab'), ('sub', 'gr...  86.9 us
    all_gather x3, blocking collectives, body(): lax.all_gather(cycle_terms, 'sub', axis=2, tiled=True)  79.3 us
    ppermute x12, starting transfers between devices, shifted(): lax.ppermute(value, axis, [(source, source + steps) for source in range(i...  41.7 us
    another operation x15, other arithmetic, gram_solve(): jnp.linalg.cholesky(matrix)  25.3 us
    another operation x10, other arithmetic, gram_solve(): jax.scipy.linalg.cho_solve((jnp.linalg.cholesky(matrix), True), right)  21.6 us
    ppermute x12, waiting for transfers between devices, shifted(): lax.ppermute(value, axis, [(source, source + steps) for source in range(i...  19.5 us
  transfers between devices with their start and end apart: 24, of which 15 were waited for; matrix products, arithmetic and copies ran while one was open for 31% of the time, Pallas kernels for 0%

commit v1 on v0

--- a/solution.py
+++ b/solution.py
@@ -79,7 +79,10 @@
             preferred_element_type=jnp.float32,
         )
         filtered = to_faces(smoothed, live_mask)
-        product = lax.psum(pair_sum(filtered, resid, "gksat,gksbt->ab"), ("sub", "grp"))
+        loads_clear = lambda m, axis_name, a_name: lax.psum(
+            lax.psum(m, axis_name), axis_name=a_name
+        )
+        product = loads_clear(pair_sum(filtered, resid, "gksat,gksbt->ab"), "grp", "sub")
         return (filtered, product)
 
     residual = loads * live_mask

time: 662 us -> 719 us (1.086); the launches traced: 658 us -> 707 us
  blocking collectives: 308 us -> 348 us
  starting transfers between devices: 47 us -> 55.3 us
    psum x2 -> x3, blocking collectives: 86.9 us -> 130 us  [body(): lax.psum(pair_sum(direction, image_faces, 'gksat,gksbt->ab'), ('sub', 'gr...]
    ppermute x12, starting transfers between devices: 41.7 us -> 49.9 us  [shifted(): lax.ppermute(value, axis, [(source, source + steps) for source in range(i...]
    psum x3 -> x6, blocking collectives: 126 us -> 120 us  [the longest x3 85.4 us: precondition(): lax.psum(lax.psum(m, axis_name), axis_name=a_name)]
  transfers between devices with their start and end apart: 24 -> 24, of which waited for: 15 -> 16; matrix products, arithmetic and copies ran while one was open for 31% -> 29% of each run, Pallas kernels for 0% -> 0%
where the time goes in v1:
time: 719 us; the launch traced here: 707 us
  blocking collectives  348 us (48%)
  local copies, waits for them, and re-layouts  194 us (27%)
  starting transfers between devices  55.3 us (8%)
  other arithmetic  49.2 us (7%)
  matrix products  30 us (4%)
  waiting for transfers between devices  28.3 us (4%)
    gather x6, local copies, waits for them, and re-layouts, body(): permute = jax.vmap(lambda matrix, ordering: matrix[ordering][:, ordering])  178 us
    psum x3, blocking collectives, body(): lax.psum(pair_sum(direction, image_faces, 'gksat,gksbt->ab'), ('sub', 'gr...  130 us
    psum x3, blocking collectives, precondition(): lax.psum(lax.psum(m, axis_name), axis_name=a_name)  85.4 us
    all_gather x3, blocking collectives, body(): lax.all_gather(cycle_terms, 'sub', axis=2, tiled=True)  82.9 us
    ppermute x12, starting transfers between devices, shifted(): lax.ppermute(value, axis, [(source, source + steps) for source in range(i...  49.9 us
    psum x3, blocking collectives, precondition(): lax.psum(m, axis_name)  34.2 us
    another operation x15, other arithmetic, gram_solve(): jnp.linalg.cholesky(matrix)  25.3 us
    another operation x10, other arithmetic, gram_solve(): jax.scipy.linalg.cho_solve((jnp.linalg.cholesky(matrix), True), right)  21.6 us
  transfers between devices with their start and end apart: 24, of which 16 were waited for; matrix products, arithmetic and copies ran while one was open for 29% of the time, Pallas kernels for 0%

profile of v1, /device:TPU:10, one launch (start us, length us, event | category | flops | bytes accessed | tf_op | source)
XLA Modules:
  0.0 707.0 jit_solution(15455465491789298326)
XLA Ops:
  7.0 42.1 %gather_fusion = bf16[2048,1024]{1,0:T(8,128)(2,1)} fusion(bf16[2,1024,1024]{2,1,0:T(8,128)(2,1)} %bitcast.533, s32[2048]{0:T(1024)S(1)} %bitcast.528), kind=kCustom, calls=%fused_computation | custom fusion | bytes 8404992 | tf_op jit(solution)/shard_map/vmap()/gather | solution.py:57
  49.1 6.2 copy.171
  55.3 40.5 %gather_fusion.1 = bf16[2048,1024]{1,0:T(8,128)(2,1)} fusion(bf16[2,1024,1024]{1,2,0:T(8,128)(2,1)} %copy.171, s32[2048]{0:T(1024)S(1)} %bitcast.529), kind=kCustom, calls=%fused_computation.1 | custom fusion | bytes 8404992 | tf_op jit(solution)/shard_map/vmap()/gather | solution.py:57
  95.9 42.1 %gather_fusion.2 = bf16[2048,1024]{1,0:T(8,128)(2,1)} fusion(bf16[2,1024,1024]{2,1,0:T(8,128)(2,1)} %bitcast.534, s32[2048]{0:T(1024)S(1)} %bitcast.530), kind=kCustom, calls=%fused_computation.2 | custom fusion | bytes 8404992 | tf_op jit(solution)/shard_map/vmap()/gather | solution.py:57
  138.0 6.2 copy.182
  144.2 40.6 %gather_fusion.3 = bf16[2048,1024]{1,0:T(8,128)(2,1)} fusion(bf16[2,1024,1024]{1,2,0:T(8,128)(2,1)} %copy.182, s32[2048]{0:T(1024)S(1)} %bitcast.531), kind=kCustom, calls=%fused_computation.3 | custom fusion | bytes 8404992 | tf_op jit(solution)/shard_map/vmap()/gather | solution.py:57
  185.1 11.1 %gather_fusion.4 = bf16[2048,12]{1,0:T(8,128)(2,1)S(1)} fusion(bf16[2,12,1024]{1,2,0:T(8,128)(2,1)S(1)} %bitcast.549, s32[2048]{0:T(1024)S(1)} %bitcast.532), kind=kCustom, calls=%fused_computation.4 | custom fusion | bytes 114688 | tf_op jit(solution)/shard_map/vmap()/gather | solution.py:60
  217.2 5.2 all_gather.18
  222.5 26.2 %all_gather.19 = f32[4,48,192]{1,2,0:T(8,128)S(1)} all-gather(f32[4,48,24]{1,2,0:T(8,128)S(1)} %all_gather.18), channel_id=1, replica_groups=mesh['sub'=8,'grp'=4] {'sub'}, dimensions={2}, use_global_device_ids=true | all-gather | bytes 165888 | tf_op jit(solution)/shard_map/all_gather | solution.py:105
  257.5 43.5 %psum.63 = f32[48,48]{0,1:T(8,128)S(1)} all-reduce(f32[48,48]{0,1:T(8,128)S(1)} %convolution_bitcast_fusion.15), channel_id=1, replica_groups=mesh['sub'=8,'grp'=4] {'sub','grp'}, use_global_device_ids=true, to_apply=%region_0.0 | all-reduce | flops 2304 | bytes 18432 | tf_op jit(solution)/shard_map/psum | solution.py:114
  310.5 10.3 %psum.64 = f32[48,48]{0,1:T(8,128)S(1)} all-reduce(f32[48,48]{0,1:T(8,128)S(1)} %convolution_bitcast_fusion.14), channel_id=1, replica_groups=mesh['sub'=8,'grp'=4] {'grp'}, use_global_device_ids=true, to_apply=%region_3.5 | all-reduce | flops 2304 | bytes 18432 | tf_op jit(solution)/shard_map/psum | solution.py:83
  320.8 27.9 %psum.65 = f32[48,48]{0,1:T(8,128)S(1)} all-reduce(f32[48,48]{0,1:T(8,128)S(1)} %psum.64), channel_id=1, replica_groups=mesh['sub'=8,'grp'=4] {'sub'}, use_global_device_ids=true, to_apply=%region_4.6 | all-reduce | flops 2304 | bytes 18432 | tf_op jit(solution)/shard_map/psum | solution.py:82
  376.1 11.9 %psum.66 = f32[48,48]{0,1:T(8,128)S(1)} all-reduce(f32[48,48]{0,1:T(8,128)S(1)} %convolution_bitcast_fusion.13), channel_id=1, replica_groups=mesh['sub'=8,'grp'=4] {'grp'}, use_global_device_ids=true, to_apply=%region_5.0 | all-reduce | flops 2304 | bytes 18432 | tf_op jit(solution)/shard_map/psum | solution.py:83
  388.0 30.1 %psum.67 = f32[48,48]{0,1:T(8,128)S(1)} all-reduce(f32[48,48]{0,1:T(8,128)S(1)} %psum.66), channel_id=1, replica_groups=mesh['sub'=8,'grp'=4] {'sub'}, use_global_device_ids=true, to_apply=%region_6.0 | all-reduce | flops 2304 | bytes 18432 | tf_op jit(solution)/shard_map/psum | solution.py:82
  441.1 5.2 all_gather.20
  446.3 28.4 %all_gather.21 = f32[4,48,192]{1,2,0:T(8,128)S(1)} all-gather(f32[4,48,24]{1,2,0:T(8,128)S(1)} %all_gather.20), channel_id=1, replica_groups=mesh['sub'=8,'grp'=4] {'sub'}, dimensions={2}, use_global_device_ids=true | all-gather | bytes 165888 | tf_op jit(solution)/shard_map/all_gather | solution.py:105
  475.7 6.0 collective-permute-start.14
  484.6 43.0 %psum.68 = f32[48,48]{0,1:T(8,128)S(1)} all-reduce(f32[48,48]{0,1:T(8,128)S(1)} %convolution_bitcast_fusion.12), channel_id=1, replica_groups=mesh['sub'=8,'grp'=4] {'sub','grp'}, use_global_device_ids=true, to_apply=%region_7.0 | all-reduce | flops 2304 | bytes 18432 | tf_op jit(solution)/shard_map/psum | solution.py:114
  555.1 12.0 %psum.69 = f32[48,48]{1,0:T(8,128)S(1)} all-reduce(f32[48,48]{1,0:T(8,128)S(1)} %convolution_bitcast_fusion.11), channel_id=1, replica_groups=mesh['sub'=8,'grp'=4] {'grp'}, use_global_device_ids=true, to_apply=%region_8.0 | all-reduce | flops 2304 | bytes 18432 | tf_op jit(solution)/shard_map/psum | solution.py:83
  567.1 27.4 %psum.70 = f32[48,48]{1,0:T(8,128)S(1)} all-reduce(f32[48,48]{1,0:T(8,128)S(1)} %psum.69), channel_id=1, replica_groups=mesh['sub'=8,'grp'=4] {'sub'}, use_global_device_ids=true, to_apply=%region_9.12 | all-reduce | flops 2304 | bytes 18432 | tf_op jit(solution)/shard_map/psum | solution.py:82
  608.1 5.2 all_gather.22
  613.3 28.3 %all_gather.23 = f32[4,48,192]{1,2,0:T(8,128)S(1)} all-gather(f32[4,48,24]{1,2,0:T(8,128)S(1)} %all_gather.22), channel_id=1, replica_groups=mesh['sub'=8,'grp'=4] {'sub'}, dimensions={2}, use_global_device_ids=true | all-gather | bytes 165888 | tf_op jit(solution)/shard_map/all_gather | solution.py:105
  642.6 6.1 collective-permute-start.22
  651.6 43.2 %psum.71 = f32[48,48]{0,1:T(8,128)S(1)} all-reduce(f32[48,48]{0,1:T(8,128)S(1)} %convolution_bitcast_fusion.10), channel_id=1, replica_groups=mesh['sub'=8,'grp'=4] {'sub','grp'}, use_global_device_ids=true, to_apply=%region_10.13 | all-reduce | flops 2304 | bytes 18432 | tf_op jit(solution)/shard_map/psum | solution.py:114
  (237 shorter events, 155.8 us)
Async XLA Ops:
  2.7 193.5 %collective-permute-start = (f32[1,48,256]{2,1,0:T(8,128)S(1)}, f32[1,48,256]{2,1,0:T(8,128)S(1)}, u32[]{:S(2)}, u32[]{:S(2)}) collective-permute-start(f32[1,48,256]{2,1,0:T(8,128)S(1)} %get-tuple-element.62), channel_id=1, source_target_pairs={{0,4},{4,8},{8,12},{12,16},{16,20},{20,24},{24,28},{1,5},{5,9},{9,... | collective-permute-start | bytes 147464 | tf_op jit(solution)/shard_map/ppermute | solution.py:15
  6.2 190.1 %collective-permute-start.1 = (f32[2,48,256]{2,1,0:T(8,128)S(1)}, f32[2,48,256]{2,1,0:T(8,128)S(1)}, u32[]{:S(2)}, u32[]{:S(2)}) collective-permute-start(f32[2,48,256]{2,1,0:T(8,128)S(1)} %slice_bitcast_fusion.5), channel_id=1, source_target_pairs={{3,0},{0,1},{1,2},{2,3},{7,4},{4,5},{5,6},{6,7},{11,8},{8,9},{9,10... | collective-permute-start | bytes 294920 | tf_op jit(solution)/shard_map/ppermute | solution.py:21
  200.2 7.1 %collective-permute-start.2 = (f32[1,48,256]{2,1,0:T(8,128)S(1)}, f32[1,48,256]{2,1,0:T(8,128)S(1)}, u32[]{:S(2)}, u32[]{:S(2)}) collective-permute-start(f32[1,48,256]{2,1,0:T(8,128)S(1)} %bitcast.587), channel_id=1, source_target_pairs={{4,0},{8,4},{12,8},{16,12},{20,16},{24,20},{28,24},{5,1},{9,5},{13... | collective-permute-start | bytes 147464 | tf_op jit(solution)/shard_map/ppermute | solution.py:15
  203.1 4.2 collective-permute-start.3
  207.4 6.3 collective-permute-start.4
  211.4 4.1 collective-permute-start.5
  249.7 6.9 collective-permute-start.6
  254.1 2.7 collective-permute-start.7
  349.9 14.2 %collective-permute-start.8 = (f32[1,48,256]{2,1,0:T(8,128)S(1)}, f32[1,48,256]{2,1,0:T(8,128)S(1)}, u32[]{:S(2)}, u32[]{:S(2)}) collective-permute-start(f32[1,48,256]{2,1,0:T(8,128)S(1)} %get-tuple-element.52), channel_id=1, source_target_pairs={{0,4},{4,8},{8,12},{12,16},{16,20},{20,24},{24,28},{1,5},{5,9},{9,... | collective-permute-start | bytes 147464 | tf_op jit(solution)/shard_map/ppermute | solution.py:15
  354.6 9.5 %collective-permute-start.9 = (f32[2,48,256]{2,1,0:T(8,128)S(1)}, f32[2,48,256]{2,1,0:T(8,128)S(1)}, u32[]{:S(2)}, u32[]{:S(2)}) collective-permute-start(f32[2,48,256]{2,1,0:T(8,128)S(1)} %slice_bitcast_fusion.3), channel_id=1, source_target_pairs={{3,0},{0,1},{1,2},{2,3},{7,4},{4,5},{5,6},{6,7},{11,8},{8,9},{9,10... | collective-permute-start | bytes 294920 | tf_op jit(solution)/shard_map/ppermute | solution.py:21
  368.0 7.1 %collective-permute-start.10 = (f32[1,48,256]{2,1,0:T(8,128)S(1)}, f32[1,48,256]{2,1,0:T(8,128)S(1)}, u32[]{:S(2)}, u32[]{:S(2)}) collective-permute-start(f32[1,48,256]{2,1,0:T(8,128)S(1)} %bitcast.589), channel_id=1, source_target_pairs={{4,0},{8,4},{12,8},{16,12},{20,16},{24,20},{28,24},{5,1},{9,5},{13... | collective-permute-start | bytes 147464 | tf_op jit(solution)/shard_map/ppermute | solution.py:15
  372.0 3.7 collective-permute-start.11
  424.1 9.0 %collective-permute-start.12 = (f32[1,48,256]{2,1,0:T(8,128)S(1)}, f32[1,48,256]{2,1,0:T(8,128)S(1)}, u32[]{:S(2)}, u32[]{:S(2)}) collective-permute-start(f32[1,48,256]{2,1,0:T(8,128)S(1)} %get-tuple-element.46), channel_id=1, source_target_pairs={{0,4},{4,8},{8,12},{12,16},{16,20},{20,24},{24,28},{1,5},{5,9},{9,... | collective-permute-start | bytes 147464 | tf_op jit(solution)/shard_map/ppermute | solution.py:15
  433.1 4.1 collective-permute-start.13
  475.7 7.7 %collective-permute-start.14 = (f32[1,48,256]{2,1,0:T(8,128)S(1)}, f32[1,48,256]{2,1,0:T(8,128)S(1)}, u32[]{:S(2)}, u32[]{:S(2)}) collective-permute-start(f32[1,48,256]{2,1,0:T(8,128)S(1)} %bitcast.590), channel_id=1, source_target_pairs={{4,0},{8,4},{12,8},{16,12},{20,16},{24,20},{28,24},{5,1},{9,5},{13... | collective-permute-start | bytes 147464 | tf_op jit(solution)/shard_map/ppermute | solution.py:15
  482.0 2.3 collective-permute-start.15
  537.9 6.0 collective-permute-start.16
  539.9 4.1 collective-permute-start.17
  547.9 6.9 collective-permute-start.18
  552.1 2.7 collective-permute-start.19
  595.3 8.6 %collective-permute-start.20 = (f32[1,48,256]{2,1,0:T(8,128)S(1)}, f32[1,48,256]{2,1,0:T(8,128)S(1)}, u32[]{:S(2)}, u32[]{:S(2)}) collective-permute-start(f32[1,48,256]{2,1,0:T(8,128)S(1)} %get-tuple-element.36), channel_id=1, source_target_pairs={{0,4},{4,8},{8,12},{12,16},{16,20},{20,24},{24,28},{1,5},{5,9},{9,... | collective-permute-start | bytes 147464 | tf_op jit(solution)/shard_map/ppermute | solution.py:15
  600.1 4.1 collective-permute-start.21
  642.6 7.9 %collective-permute-start.22 = (f32[1,48,256]{2,1,0:T(8,128)S(1)}, f32[1,48,256]{2,1,0:T(8,128)S(1)}, u32[]{:S(2)}, u32[]{:S(2)}) collective-permute-start(f32[1,48,256]{2,1,0:T(8,128)S(1)} %bitcast.592), channel_id=1, source_target_pairs={{4,0},{8,4},{12,8},{16,12},{20,16},{24,20},{28,24},{5,1},{9,5},{13... | collective-permute-start | bytes 147464 | tf_op jit(solution)/shard_map/ppermute | solution.py:15
  649.0 2.3 collective-permute-start.23
  (3 other events, 304.1 us)
